TPU v7x, 128 devices: a whole 4x4x4 slice. The times are simulated.
128 devices in a mesh: depth: 4 (over y), tile: 32 (over z, x, core).
Axes of the slice: x: 4, y: 4, z: 4, core: 2. Of those that a mesh axis runs over, the one named last changes fastest.
Arguments:
- specimen: float32 [2, 4, 8192, 4096], P(None, 'depth', 'tile'), may hold values from -0.35 to 1.1
- positions: int32 [2, 128], P(None, 'tile'), may hold values from 0 to 7936, as said below
- occupied: int32 [128], P('tile'), may hold values from 0 to 1, as said below
- measured: float32 [128, 256, 256], P('tile'), may hold values from 0.2 to 2
- probe_wave: float32 [2, 256, 256], replicated, may hold values from -4 to 4
Outputs:
- gradient: float32 [2, 4, 8192, 4096], P(None, 'depth', 'tile')
Inputs may be any that keep to these rules, and one draw needn't show every extreme that they name: `positions`: column p holds the top row and left column of patch p; the row lies from (p // 4) * 256 to that plus 256 - 1 and never past 8192 - 256; the column lies from 0 to 3840. `occupied`: each aligned block of 4 slots holds 1 to 4 ones, first in the block, then zeros; some block is all ones.
All inputs are finite; a program needn't handle non-finite values.
Results may differ from a plain program's by a relative error of at most 0.0003.
Values sent between devices are 32-bit elements; how exact they have to be, the bound alone decides.
A program may use at most 192 MiB of HBM per device.

v0:
```python
import math

import jax
import jax.numpy as jnp
from jax import lax
from jax.sharding import PartitionSpec as P

PRECISE = lax.Precision.HIGHEST


def from_behind(value, axis, steps):
    count = lax.axis_size(axis)
    first, last = (max(0, -steps), min(count, count - steps))
    return lax.ppermute(value, axis, [(source, source + steps) for source in range(first, last)])


def indices(*values):
    return tuple((jnp.asarray(value).astype(jnp.int32) for value in values))


def as_index(value):
    return jnp.asarray(value)


def product(left_side, right_side):
    return jnp.matmul(left_side, right_side, precision=PRECISE)


def complex_times(first_pair, second_pair):
    return (
        first_pair[0] * second_pair[0] - first_pair[1] * second_pair[1],
        first_pair[0] * second_pair[1] + first_pair[1] * second_pair[0],
    )


def conjugate(pair):
    return (pair[0], -pair[1])


def transposed(pair):
    return (pair[0].T, pair[1].T)


def complex_left(matrix, values):
    return (
        product(matrix[0], values[0]) - product(matrix[1], values[1]),
        product(matrix[0], values[1]) + product(matrix[1], values[0]),
    )


def complex_right(values, matrix):
    return (
        product(values[0], matrix[0]) - product(values[1], matrix[1]),
        product(values[0], matrix[1]) + product(values[1], matrix[0]),
    )


def sandwich(left_table, values, right_table):
    return complex_right(complex_left(left_table, values), right_table)


def transform_tables(length):
    counter = jnp.arange(length, dtype=jnp.int32)
    phase_grid = (
        2.0 * math.pi / length * (counter[:, None] * counter[None, :] % length).astype(jnp.float32)
    )
    norm_factor = 1.0 / math.sqrt(length)
    unitary = (jnp.cos(phase_grid) * norm_factor, -jnp.sin(phase_grid) * norm_factor)
    centred = ((counter + length // 2) % length - length // 2).astype(jnp.float32)
    fresnel = -12.0 * centred * centred / (length * length)
    filter_re = jnp.cos(fresnel)[:, None]
    filter_im = jnp.sin(fresnel)[:, None]
    filtered = (
        filter_re * unitary[0] - filter_im * unitary[1],
        filter_re * unitary[1] + filter_im * unitary[0],
    )
    kernel = complex_left(conjugate(unitary), filtered)
    return (unitary, kernel)


def propagate(values, kernel):
    return sandwich(kernel, values, transposed(kernel))


def propagate_back(values, kernel):
    return sandwich(transposed(conjugate(kernel)), values, conjugate(kernel))


def far_residual(values, unitary, target):
    far_field = sandwich(unitary, values, transposed(unitary))
    excess = far_field[0] * far_field[0] + far_field[1] * far_field[1] - target
    scaled = (excess * far_field[0], excess * far_field[1])
    return sandwich(transposed(conjugate(unitary)), scaled, conjugate(unitary))


def local(specimen, positions, occupied, measured, probe_wave):
    depth_count = lax.axis_size("depth")
    depth_index = as_index(lax.axis_index("depth"))
    tile_index = as_index(lax.axis_index("tile"))
    patch_size = probe_wave.shape[-1]
    slot_count = occupied.shape[0]
    strip_rows = specimen.shape[2]
    unitary, kernel = transform_tables(patch_size)
    own_strip = specimen[:, 0]
    row_local = positions[0] - tile_index * strip_rows
    col_start = positions[1]
    weights = occupied.astype(jnp.float32)

    def cut_patch(source, row_offset, col_offset):
        return lax.dynamic_slice(
            source, indices(0, row_offset, col_offset), (2, patch_size, patch_size)
        )

    borrowed = from_behind(own_strip, "tile", -1)
    window = jnp.concatenate([own_strip, borrowed], axis=1)
    transmit = jax.vmap(lambda row_offset, col_offset: cut_patch(window, row_offset, col_offset))(
        row_local, col_start
    )
    group_count = 1
    group_size = slot_count // group_count
    steps_total = depth_count + group_count - 1
    probe_block = jnp.broadcast_to(probe_wave[:, None], (2, group_size, patch_size, patch_size))
    saved_waves = jnp.zeros((2, slot_count, patch_size, patch_size), jnp.float32)
    arriving = jnp.zeros_like(probe_block)

    def resting():
        return jnp.zeros_like(probe_block)

    for step_number in range(steps_total):
        group_index = step_number - depth_index
        active = (group_index >= 0) & (group_index < group_count)
        incoming = jnp.where(depth_index == 0, probe_block, arriving)
        previous = saved_waves
        saved_waves = jnp.where(active, incoming, previous)
        tiles_now = transmit

        def advance():
            passed = complex_times((tiles_now[:, 0], tiles_now[:, 1]), (incoming[0], incoming[1]))
            return jnp.stack(propagate(passed, kernel))

        leaving = lax.cond(active & (depth_index < depth_count - 1), advance, resting)
        arriving = from_behind(leaving, "depth", 1)
    patch_grads = jnp.zeros((slot_count, 2, patch_size, patch_size), jnp.float32)
    arriving = jnp.zeros_like(probe_block)
    for step_number in range(steps_total):
        group_index = step_number - (depth_count - 1 - depth_index)
        active = (group_index >= 0) & (group_index < group_count)
        waves_now = saved_waves
        tiles_now = transmit

        def from_detector():
            passed = complex_times((tiles_now[:, 0], tiles_now[:, 1]), (waves_now[0], waves_now[1]))
            return jnp.stack(far_residual(passed, unitary, measured))

        def from_below():
            return arriving

        adjoint = lax.cond(active & (depth_index == depth_count - 1), from_detector, from_below)
        contribution = complex_times(
            conjugate((waves_now[0], waves_now[1])), (adjoint[0], adjoint[1])
        )
        scaled = jnp.stack(contribution, axis=1) * weights[:, None, None, None]
        previous = patch_grads
        patch_grads = jnp.where(active, scaled, previous)

        def retreat():
            reflected = complex_times(
                conjugate((tiles_now[:, 0], tiles_now[:, 1])), (adjoint[0], adjoint[1])
            )
            return jnp.stack(propagate_back(reflected, kernel))

        leaving = lax.cond(active & (depth_index > 0), retreat, resting)
        arriving = from_behind(leaving, "depth", -1)

    def place_wide(slot_number, canvas):
        row_offset = row_local[slot_number]
        col_offset = col_start[slot_number]
        existing = cut_patch(canvas, row_offset, col_offset)
        return lax.dynamic_update_slice(
            canvas, existing + patch_grads[slot_number], indices(0, row_offset, col_offset)
        )

    canvas = lax.fori_loop(
        0,
        slot_count,
        place_wide,
        jnp.zeros((2, strip_rows + patch_size, own_strip.shape[2]), jnp.float32),
    )
    spilled = from_behind(canvas[:, strip_rows:], "tile", 1)
    gradient_strip = canvas[:, :strip_rows].at[:, :patch_size].add(spilled)
    return gradient_strip[:, None]


def solution(mesh):
    placed = (
        P(None, "depth", "tile", None),
        P(None, "tile"),
        P("tile"),
        P("tile", None, None),
        P(),
    )
    return jax.shard_map(
        local, mesh=mesh, in_specs=placed, out_specs=P(None, "depth", "tile", None), check_vma=False
    )
```

profile of v0, /device:TPU:1, one launch (start us, length us, event | category | flops | bytes accessed | tf_op | source)
XLA Modules:
  0.0 787.4 jit_solution(15203871150859333828)
XLA Ops:
  11.6 84.4 %collective-permute-done = f32[2,256,4096]{2,1,0:T(8,128)} collective-permute-done((f32[2,256,4096]{2,1,0:T(8,128)}, f32[2,256,4096]{2,1,0:T(8,128)}, u32[]{:S(2)}, u32[]{:S(2)}) %collective-permute-start) | collective-permute-done | bytes 8388640 | tf_op jit(solution)/shard_map/ppermute | solution.py:14
  95.9 10.0 %pad_maximum_fusion.9 = f32[2,512,4096]{2,1,0:T(8,128)} fusion(f32[2,256,4096]{2,1,0:T(8,128)} %collective-permute-done, f32[2,256,4096]{2,1,0:T(8,128)S(1)} %bitcast.862), kind=kLoop, calls=%fused_computation.387 | loop fusion | flops 4194304 | bytes 33554432 | tf_op jit(solution)/shard_map/concatenate | solution.py:115
  106.0 16.3 %while.19 = (s32[]{:T(128)}, f32[2,512,4096]{2,1,0:T(8,128)}, s32[4,3]{1,0:T(4,128)S(1)}, f32[4,2,256,256]{3,2,1,0:T(8,128)}) while((s32[]{:T(128)}, f32[2,512,4096]{2,1,0:T(8,128)}, s32[4,3]{1,0:T(4,128)S(1)}, f32[4,2,256,256]{3,2,1,0:T(8,128)}) %tuple.199), condition=%wide.while_cond.1.clone, body=%wide.while_body.1.sunk.clone | while | flops 2 | bytes 1049709 | solution.py:110
  106.6 3.4 bitcast_dynamic-update-slice_fusion.3
  122.3 18.1 %conditional.10 = (f32[2,4,256,256]{3,2,1,0:T(8,128)}) conditional(s32[]{:T(128)} %convert_element_type.196, () %tuple.120, (f32[4,2,256,256]{3,2,1,0:T(8,128)}, f32[2,256,256]{1,2,0:T(8,128)S(1)}, f32[256,256]{1,0:T(8,128)S(1)}, f32[256,256]{1,0:T(8,128)S(1)}) %tuple.121), branch_computations={%region_0.1_spmd, %region_1.2_spmd} | conditional | flops 6447169536 | bytes 47185956 | solution.py:141
  143.1 29.9 %collective-permute-done.1 = f32[2,4,256,256]{3,2,1,0:T(8,128)} collective-permute-done((f32[2,4,256,256]{3,2,1,0:T(8,128)}, f32[2,4,256,256]{3,2,1,0:T(8,128)}, u32[]{:S(2)}, u32[]{:S(2)}) %collective-permute-start.1) | collective-permute-done | bytes 2097184 | tf_op jit(solution)/shard_map/ppermute | solution.py:14
  174.5 9.3 %conditional.11 = (f32[2,4,256,256]{3,2,1,0:T(8,128)}) conditional(s32[]{:T(128)} %convert_element_type.195, () %tuple.119, (f32[4,2,256,256]{3,2,1,0:T(8,128)}, f32[2,4,256,256]{3,2,1,0:T(8,128)}, f32[256,256]{1,0:T(8,128)S(1)}, f32[256,256]{1,0:T(8,128)S(1)}) %tuple.122), branch_computations={%region_2.3_spmd, %region_3.4_spmd} | conditional | flops 6445596672 | bytes 41943048 | solution.py:141
  183.8 19.7 %collective-permute-start.2 = (f32[2,4,256,256]{3,2,1,0:T(8,128)}, f32[2,4,256,256]{3,2,1,0:T(8,128)}, u32[]{:S(2)}, u32[]{:S(2)}) collective-permute-start(f32[2,4,256,256]{3,2,1,0:T(8,128)} %get-tuple-element.793), channel_id=1, source_target_pairs={{0,32},{32,64},{64,96},{1,33},{33,65},{65,97},{2,34},{34,66},{66,9... | collective-permute-start | bytes 6291464 | tf_op jit(solution)/shard_map/ppermute | solution.py:14
  203.4 21.9 %collective-permute-done.2 = f32[2,4,256,256]{3,2,1,0:T(8,128)} collective-permute-done((f32[2,4,256,256]{3,2,1,0:T(8,128)}, f32[2,4,256,256]{3,2,1,0:T(8,128)}, u32[]{:S(2)}, u32[]{:S(2)}) %collective-permute-start.2) | collective-permute-done | bytes 2097184 | tf_op jit(solution)/shard_map/ppermute | solution.py:14
  228.7 6.7 collective-permute-start.3
  239.6 17.8 %collective-permute-done.3 = f32[2,4,256,256]{3,2,1,0:T(8,128)} collective-permute-done((f32[2,4,256,256]{3,2,1,0:T(8,128)}, f32[2,4,256,256]{3,2,1,0:T(8,128)}, u32[]{:S(2)}, u32[]{:S(2)}) %collective-permute-start.3) | collective-permute-done | bytes 2097184 | tf_op jit(solution)/shard_map/ppermute | solution.py:14
  262.2 12.6 %conditional.13 = (f32[2,4,256,256]{3,2,1,0:T(8,128)}, f32[4,1,256,256]{3,2,0,1:T(8,128)}, f32[4,1,256,256]{3,2,0,1:T(8,128)}) conditional(s32[]{:T(128)} %convert_element_type.205, () %tuple.127, (f32[4,2,256,256]{2,3,0,1:T(8,128)}, f32[2,4,256,256]{2,3,1,0:T(8,128)}, f32[256,256]{1,0:T(8,128)S(1)}, f32[256,256]{1,0:T(8,128)S(1)}, ...), branch_computations={%region_6.7_spmd, %region_7.8_spmd} | conditional | flops 12894601216 | bytes 65011736 | solution.py:158
  274.8 8.9 %conditional.14 = (f32[2,4,256,256]{3,2,1,0:T(8,128)}) conditional(s32[]{:T(128)} %convert_element_type.204, () %tuple.126, (f32[4,2,256,256]{3,2,1,0:T(8,128)}, f32[2,4,256,256]{3,2,1,0:T(8,128)}, f32[256,256]{1,0:T(8,128)S(1)}, f32[256,256]{1,0:T(8,128)S(1)}) %tuple.129), branch_computations={%region_8.9_spmd, %region_9.10_spmd} | conditional | flops 6446120960 | bytes 41943048 | solution.py:172
  285.1 63.4 %collective-permute-done.4 = f32[2,4,256,256]{3,2,1,0:T(8,128)} collective-permute-done((f32[2,4,256,256]{3,2,1,0:T(8,128)}, f32[2,4,256,256]{3,2,1,0:T(8,128)}, u32[]{:S(2)}, u32[]{:S(2)}) %collective-permute-start.4) | collective-permute-done | bytes 2097184 | tf_op jit(solution)/shard_map/ppermute | solution.py:14
  348.5 11.9 %conditional.15 = (f32[2,4,256,256]{3,2,1,0:T(8,128)}, f32[4,1,256,256]{3,2,0,1:T(8,128)}, f32[4,1,256,256]{3,2,0,1:T(8,128)}) conditional(s32[]{:T(128)} %convert_element_type.203, f32[2,4,256,256]{3,2,1,0:T(8,128)} %collective-permute-done.4, (f32[4,2,256,256]{2,3,0,1:T(8,128)}, f32[2,4,256,256]{2,3,1,0:T(8,128)}, f32[256,256]{1,0:T(8,128)S(1)}, ...), branch_computations={%region_10.11_spmd, %region_11.12_spmd} | conditional | flops 12894601216 | bytes 65011736 | solution.py:158
  360.3 8.7 %conditional.16 = (f32[2,4,256,256]{3,2,1,0:T(8,128)}) conditional(s32[]{:T(128)} %convert_element_type.202, () %tuple.125, (f32[4,2,256,256]{3,2,1,0:T(8,128)}, f32[2,4,256,256]{3,2,1,0:T(8,128)}, f32[256,256]{1,0:T(8,128)S(1)}, f32[256,256]{1,0:T(8,128)S(1)}) %tuple.130), branch_computations={%region_12.13_spmd, %region_13.14_spmd} | conditional | flops 6446120960 | bytes 41943048 | solution.py:172
  370.4 25.8 %collective-permute-done.5 = f32[2,4,256,256]{3,2,1,0:T(8,128)} collective-permute-done((f32[2,4,256,256]{3,2,1,0:T(8,128)}, f32[2,4,256,256]{3,2,1,0:T(8,128)}, u32[]{:S(2)}, u32[]{:S(2)}) %collective-permute-start.5) | collective-permute-done | bytes 2097184 | tf_op jit(solution)/shard_map/ppermute | solution.py:14
  396.1 12.0 %conditional.17 = (f32[2,4,256,256]{3,2,1,0:T(8,128)}, f32[4,1,256,256]{3,2,0,1:T(8,128)}, f32[4,1,256,256]{3,2,0,1:T(8,128)}) conditional(s32[]{:T(128)} %convert_element_type.201, f32[2,4,256,256]{3,2,1,0:T(8,128)} %collective-permute-done.5, (f32[4,2,256,256]{2,3,0,1:T(8,128)}, f32[2,4,256,256]{2,3,1,0:T(8,128)}, f32[256,256]{1,0:T(8,128)S(1)}, ...), branch_computations={%region_14.15_spmd, %region_15.16_spmd} | conditional | flops 12894601216 | bytes 65011736 | solution.py:158
  408.1 9.7 %conditional.18 = (f32[2,4,256,256]{3,2,1,0:T(8,128)}) conditional(s32[]{:T(128)} %convert_element_type.200, () %tuple.124, (f32[4,2,256,256]{3,2,1,0:T(8,128)}, f32[2,4,256,256]{3,2,1,0:T(8,128)}, f32[256,256]{1,0:T(8,128)S(1)}, f32[256,256]{1,0:T(8,128)S(1)}) %tuple.131), branch_computations={%region_16.17_spmd, %region_17.18_spmd} | conditional | flops 6446120960 | bytes 41943048 | solution.py:172
  419.2 6.5 fusion.278
  425.7 94.5 %collective-permute-done.6 = f32[2,4,256,256]{3,2,1,0:T(8,128)} collective-permute-done((f32[2,4,256,256]{3,2,1,0:T(8,128)}, f32[2,4,256,256]{3,2,1,0:T(8,128)}, u32[]{:S(2)}, u32[]{:S(2)}) %collective-permute-start.6) | collective-permute-done | bytes 2097184 | tf_op jit(solution)/shard_map/ppermute | solution.py:14
  520.2 6.0 conditional.19
  531.3 7.9 %broadcast_in_dim.35 = f32[2,512,4096]{2,1,0:T(8,128)} broadcast(f32[]{:T(128)} %constant.129.clone.1), dimensions={} | broadcast | bytes 16777220 | tf_op jit(solution)/shard_map/broadcast_in_dim | solution.py:187
  539.2 50.6 %while.18 = (s32[]{:T(128)}, f32[2,512,4096]{2,1,0:T(8,128)}, s32[4]{0:T(128)S(1)}, s32[4]{0:T(128)S(1)}, f32[4,2,256,256]{3,2,1,0:T(8,128)}) while((s32[]{:T(128)}, f32[2,512,4096]{2,1,0:T(8,128)}, s32[4]{0:T(128)S(1)}, s32[4]{0:T(128)S(1)}, f32[4,2,256,256]{3,2,1,0:T(8,128)}) %tuple.210), condition=%wide.region_21.22_spmd.clone, body=%wide.region_20.21_spmd.sunk.clone | while | flops 131080 | bytes 2621617 | solution.py:183
  545.3 6.1 dynamic_update_slice.9
  557.5 6.7 dynamic_update_slice.9
  570.3 6.7 dynamic_update_slice.9
  583.2 6.6 dynamic_update_slice.9
  589.8 3.9 slice.238
  593.7 91.8 %collective-permute-start.7 = (f32[2,256,4096]{2,1,0:T(8,128)S(1)}, f32[2,256,4096]{2,1,0:T(8,128)}, u32[]{:S(2)}, u32[]{:S(2)}) collective-permute-start(f32[2,256,4096]{2,1,0:T(8,128)S(1)} %slice.238), channel_id=1, source_target_pairs={{0,1},{1,2},{2,3},{3,4},{4,5},{5,6},{6,7},{7,8},{8,9},{9,10},{10,1... | collective-permute-start | bytes 25165832 | tf_op jit(solution)/shard_map/ppermute | solution.py:14
  685.5 90.4 %collective-permute-done.7 = f32[2,256,4096]{2,1,0:T(8,128)} collective-permute-done((f32[2,256,4096]{2,1,0:T(8,128)S(1)}, f32[2,256,4096]{2,1,0:T(8,128)}, u32[]{:S(2)}, u32[]{:S(2)}) %collective-permute-start.7) | collective-permute-done | bytes 8388640 | tf_op jit(solution)/shard_map/ppermute | solution.py:14
  775.9 11.3 %add_bitcast_fusion = f32[2,1,256,4096]{3,2,1,0:T(8,128)} fusion(f32[2,256,4096]{2,1,0:T(8,128)} %collective-permute-done.7, f32[2,512,4096]{2,1,0:T(8,128)} %get-tuple-element.475), kind=kLoop, calls=%fused_computation.388 | loop fusion | flops 2097152 | bytes 25165824 | tf_op jit(solution)/shard_map/broadcast_in_dim | solution.py:191
  (100 shorter events, 97.7 us)
Async XLA Ops:
  0.0 95.9 %collective-permute-start = (f32[2,256,4096]{2,1,0:T(8,128)}, f32[2,256,4096]{2,1,0:T(8,128)}, u32[]{:S(2)}, u32[]{:S(2)}) collective-permute-start(f32[2,256,4096]{2,1,0:T(8,128)} %bitcast.861), channel_id=1, source_target_pairs={{1,0},{2,1},{3,2},{4,3},{5,4},{6,5},{7,6},{8,7},{9,8},{10,9},{11,1... | collective-permute-start | bytes 25165832 | tf_op jit(solution)/shard_map/ppermute | solution.py:14
  7.0 88.9 %copy-start.5 = (f32[2,1,256,4096]{3,2,1,0:T(8,128)S(1)}, f32[2,1,256,4096]{3,2,1,0:T(8,128)}, u32[]{:S(2)}) copy-start(f32[2,1,256,4096]{3,2,1,0:T(8,128)} %param.31) | copy-start | bytes 25165828
  122.3 50.6 %copy-start.4 = (f32[2,256,256]{2,1,0:T(8,128)S(1)}, f32[2,256,256]{2,1,0:T(8,128)}, u32[]{:S(2)}) copy-start(f32[2,256,256]{2,1,0:T(8,128)} %param.35) | copy-start | bytes 1572868
  125.4 2.7 copy-start.3
  140.4 32.5 %collective-permute-start.1 = (f32[2,4,256,256]{3,2,1,0:T(8,128)}, f32[2,4,256,256]{3,2,1,0:T(8,128)}, u32[]{:S(2)}, u32[]{:S(2)}) collective-permute-start(f32[2,4,256,256]{3,2,1,0:T(8,128)} %get-tuple-element.792), channel_id=1, source_target_pairs={{0,32},{32,64},{64,96},{1,33},{33,65},{65,97},{2,34},{34,66},{66,9... | collective-permute-start | bytes 6291464 | tf_op jit(solution)/shard_map/ppermute | solution.py:14
  183.8 41.6 %collective-permute-start.2 = (f32[2,4,256,256]{3,2,1,0:T(8,128)}, f32[2,4,256,256]{3,2,1,0:T(8,128)}, u32[]{:S(2)}, u32[]{:S(2)}) collective-permute-start(f32[2,4,256,256]{3,2,1,0:T(8,128)} %get-tuple-element.793), channel_id=1, source_target_pairs={{0,32},{32,64},{64,96},{1,33},{33,65},{65,97},{2,34},{34,66},{66,9... | collective-permute-start | bytes 6291464 | tf_op jit(solution)/shard_map/ppermute | solution.py:14
  228.7 28.7 %collective-permute-start.3 = (f32[2,4,256,256]{3,2,1,0:T(8,128)}, f32[2,4,256,256]{3,2,1,0:T(8,128)}, u32[]{:S(2)}, u32[]{:S(2)}) collective-permute-start(f32[2,4,256,256]{3,2,1,0:T(8,128)} %get-tuple-element.794), channel_id=1, source_target_pairs={{0,32},{32,64},{64,96},{1,33},{33,65},{65,97},{2,34},{34,66},{66,9... | collective-permute-start | bytes 6291464 | tf_op jit(solution)/shard_map/ppermute | solution.py:14
  259.2 3.0 copy-start
  283.8 64.7 %collective-permute-start.4 = (f32[2,4,256,256]{3,2,1,0:T(8,128)}, f32[2,4,256,256]{3,2,1,0:T(8,128)}, u32[]{:S(2)}, u32[]{:S(2)}) collective-permute-start(f32[2,4,256,256]{3,2,1,0:T(8,128)} %get-tuple-element.795), channel_id=1, source_target_pairs={{32,0},{64,32},{96,64},{33,1},{65,33},{97,65},{34,2},{66,34},{98,6... | collective-permute-start | bytes 6291464 | tf_op jit(solution)/shard_map/ppermute | solution.py:14
  369.0 27.1 %collective-permute-start.5 = (f32[2,4,256,256]{3,2,1,0:T(8,128)}, f32[2,4,256,256]{3,2,1,0:T(8,128)}, u32[]{:S(2)}, u32[]{:S(2)}) collective-permute-start(f32[2,4,256,256]{3,2,1,0:T(8,128)} %get-tuple-element.796), channel_id=1, source_target_pairs={{32,0},{64,32},{96,64},{33,1},{65,33},{97,65},{34,2},{66,34},{98,6... | collective-permute-start | bytes 6291464 | tf_op jit(solution)/shard_map/ppermute | solution.py:14
  408.1 11.0 %copy-start.12 = (s32[4]{0:T(128)S(1)}, s32[4]{0:T(128)}, u32[]{:S(2)}) copy-start(s32[4]{0:T(128)} %param.33) | copy-start | bytes 52
  408.1 11.0 %copy-start.11 = (s32[2,4]{1,0:T(2,128)S(1)}, s32[2,4]{1,0:T(2,128)}, u32[]{:S(2)}) copy-start(s32[2,4]{1,0:T(2,128)} %param.32) | copy-start | bytes 100
  417.8 102.4 %collective-permute-start.6 = (f32[2,4,256,256]{3,2,1,0:T(8,128)}, f32[2,4,256,256]{3,2,1,0:T(8,128)}, u32[]{:S(2)}, u32[]{:S(2)}) collective-permute-start(f32[2,4,256,256]{3,2,1,0:T(8,128)} %get-tuple-element.797), channel_id=1, source_target_pairs={{32,0},{64,32},{96,64},{33,1},{65,33},{97,65},{34,2},{66,34},{98,6... | collective-permute-start | bytes 6291464 | tf_op jit(solution)/shard_map/ppermute | solution.py:14
  419.2 6.5 copy-start.1
  419.2 6.5 copy-start.2
  526.2 2.2 copy-start.6
  526.2 2.2 copy-start.7
  526.2 2.5 copy-start.8
  526.2 2.8 copy-start.9
  526.2 3.1 copy-start.10
  593.7 182.2 %collective-permute-start.7 = (f32[2,256,4096]{2,1,0:T(8,128)S(1)}, f32[2,256,4096]{2,1,0:T(8,128)}, u32[]{:S(2)}, u32[]{:S(2)}) collective-permute-start(f32[2,256,4096]{2,1,0:T(8,128)S(1)} %slice.238), channel_id=1, source_target_pairs={{0,1},{1,2},{2,3},{3,4},{4,5},{5,6},{6,7},{7,8},{8,9},{9,10},{10,1... | collective-permute-start | bytes 25165832 | tf_op jit(solution)/shard_map/ppermute | solution.py:14
where the time goes:
time: 796 us; the launch traced here: 787 us
  waiting for transfers between devices  428 us (54%)
  starting transfers between devices  128 us (16%)
  local copies, waits for them, and re-layouts  89.7 us (11%)
  loops' own time  75.4 us (9%)
  other arithmetic  46.4 us (6%)
  matrix products  19.3 us (2%)
    ppermute x8, waiting for transfers between devices, from_behind(): lax.ppermute(value, axis, [(source, source + steps) for source in range(f...  428 us
    ppermute x8, starting transfers between devices, from_behind(): lax.ppermute(value, axis, [(source, source + steps) for source in range(f...  128 us
    another operation x4, loops' own time, local(): lax.cond(active & (depth_index == depth_count - 1), from_detector, from_b...  30.9 us
    dynamic_update_slice x4, local copies, waits for them, and re-layouts, place_wide(): lax.dynamic_update_slice(canvas, existing + patch_grads[slot_number], ind...  26.2 us
    another operation x3, loops' own time, local(): leaving = lax.cond(active & (depth_index > 0), retreat, resting)  22.8 us
    dot_general x12, matrix products, product(): return jnp.matmul(left_side, right_side, precision=PRECISE)  19.3 us
    gather x12, local copies, waits for them, and re-layouts  16.3 us
  transfers between devices with their start and end apart: 8, of which 8 were waited for; matrix products, arithmetic and copies ran while one was open for 2% of the time, Pallas kernels for 0%

commit v1 on v0

v1 whole, which is shorter than its diff:
```python
import functools
import math

import jax
import jax.numpy as jnp
import ml_dtypes
import numpy as np
from jax import lax
from jax.experimental import pallas as pl
from jax.experimental.pallas import tpu as pltpu
from jax.sharding import PartitionSpec as P

MESH = pl.DeviceIdType.MESH
BF = jnp.bfloat16
F32 = jnp.float32
N = 256
H = 128
PIECE = (2, N, N)


def transform_tables():
    j = np.arange(N)
    unitary = np.exp(-2j * np.pi * ((j[:, None] * j[None, :]) % N) / N) / math.sqrt(N)
    f = ((j + H) % N) - H
    kernel = np.conj(unitary) @ (np.exp(-12j * f * f / (N * N))[:, None] * unitary)
    kernels = [(kernel[:H, :H] + sign * kernel[:H, H:]) / 2 for sign in (1, -1)]
    halves = [unitary[:H, 0::2], unitary[:H, 1::2]]

    def left(m):
        return np.block([[m.real, -m.imag], [m.imag, m.real]])

    def right(m):
        return np.block([[m.real, m.imag], [-m.imag, m.real]])

    lefts = [[left(m) for m in kernels], [left(m.T) for m in halves], [left(m) for m in halves]]
    rights = [[right(m) for m in kernels], [right(m) for m in halves], [right(m.T) for m in halves]]
    exact = np.array([lefts, rights])
    high = exact.astype(ml_dtypes.bfloat16)
    low = (exact - high.astype(np.float64)).astype(ml_dtypes.bfloat16)
    return np.stack([high, low], axis=3)


def order_table():
    table = np.zeros((N, N))
    table[np.arange(N), np.r_[0:N:2, 1:N:2]] = 1
    return table.astype(ml_dtypes.bfloat16)


def split(x):
    high = x.astype(BF)
    return high, (x - high.astype(F32)).astype(BF)


def dot(a, b):
    return jnp.dot(a, b, preferred_element_type=F32)


def exact_dot(multiply, x):
    high = x.astype(BF)
    rest = x - high.astype(F32)
    middle = rest.astype(BF)
    low = (rest - middle.astype(F32)).astype(BF)
    return multiply(high) + (multiply(middle) + multiply(low))


def put(buf, index, rows, cols, x):
    high, low = split(x)
    buf[index, 0, rows, cols] = high
    buf[index, 1, rows, cols] = low


def half(i):
    return slice(i * H, (i + 1) * H)


def butterfly_store(xr, xi, dbuf):
    for c, x in ((0, xr), (1, xi)):
        top, bottom = x[:H], x[H:]
        for a, y in ((0, top + bottom), (1, top - bottom)):
            put(dbuf, a, half(c), half(0), y[:, :H] + y[:, H:])
            put(dbuf, a, half(c), half(1), y[:, :H] - y[:, H:])


def left_product(kind, tab, dbuf, ebuf):
    for a in range(2):
        high, low = dbuf[a, 0], dbuf[a, 1]
        e = dot(tab[0, kind, a, 0], high) + (dot(tab[0, kind, a, 0], low) + dot(tab[0, kind, a, 1], high))
        for c in range(2):
            for b in range(2):
                put(ebuf, b, half(a), half(c), e[half(c), half(b)])


def right_product(kind, tab, ebuf):
    out = []
    for b in range(2):
        high, low = ebuf[b, 0], ebuf[b, 1]
        out.append(dot(high, tab[1, kind, b, 0]) + (dot(low, tab[1, kind, b, 0]) + dot(high, tab[1, kind, b, 1])))
    return out


def unbutterfly(g):
    res = []
    for c in range(2):
        p, m = g[0][:, half(c)], g[1][:, half(c)]
        y = jnp.concatenate([p + m, p - m], axis=1)
        res.append(jnp.concatenate([y[:H] + y[H:], y[:H] - y[H:]], axis=0))
    return res


def cut(spec, row, col, top, store):
    block = lax.div(col, H)
    rem = lax.rem(col, H)
    odd = lax.rem(block, 2)
    chunk = 32

    def body(i, _):
        rows = pl.ds(pl.multiple_of(i * chunk, chunk), chunk)
        lane = lax.broadcasted_iota(jnp.int32, (chunk, H), 1)
        line = lax.broadcasted_iota(jnp.int32, (chunk, H), 0) + i * chunk
        keep = line >= row if top else line < row
        for side in range(2):
            first = block + (odd if side == 0 else 1 - odd)
            second = first + 2 - 2 * lax.div(first + 2, 32)
            limit = rem * (1 - odd if side == 0 else odd)
            for c in range(2):
                here = spec[first, c, rows, :]
                there = spec[second, c, rows, :]
                store(c, rows, half(side), jnp.where(keep, jnp.where(lane >= limit, here, there), 0.0))
        return 0

    lax.fori_loop(0, N // chunk, body, 0)


def gradient_pieces(
    depth, tiles, specimen, positions, occupied, measured, probe, tables, order,
    own_out, spill_out, before_out,
    spec, mine, halo_out, halo_in, merged, waves, psi, g, dbuf, ebuf, grads, grads_in, tab, perm, meas, mp, wave0,
    pos1, pos2, occ2,
    load_sem, spec_sem, info_send, info_recv, halo_send, halo_recv, far_send, far_recv, y_send, y_recv,
    g_send, g_recv, spill_send, spill_recv, back_send, back_recv, meas_send, meas_recv, out_sem,
):
    d = lax.axis_index("depth")
    t = lax.axis_index("tile")
    odd = lax.rem(t, 2)

    def tile(k):
        return lax.rem(t + k + tiles, tiles)

    def level(k):
        return lax.rem(d + k, depth)

    def remote(src, dst, send, recv, to):
        return pltpu.make_async_remote_copy(
            src_ref=src, dst_ref=dst, send_sem=send, recv_sem=recv, device_id=to, device_id_type=MESH
        )

    far_slot = (odd == 1) & (d >= 2)

    loads = [
        pltpu.make_async_copy(probe, wave0, load_sem.at[0]),
        pltpu.make_async_copy(order, perm, load_sem.at[1]),
        pltpu.make_async_copy(tables, tab, load_sem.at[2]),
    ]
    meas_load = pltpu.make_async_copy(measured.at[d], meas, load_sem.at[3])
    for copy in loads[:2]:
        copy.start()

    @pl.when(jnp.logical_not(far_slot))
    def _():
        meas_load.start()

    def block_load(b):
        cols = pl.ds(pl.multiple_of(b * H, H), H)
        return pltpu.make_async_copy(specimen.at[:, 0, :, cols], spec.at[b], spec_sem.at[b])

    blocks = spec.shape[0]
    lax.fori_loop(0, blocks, lambda b, _: (block_load(b).start(), 0)[1], 0)
    loads[2].start()

    barrier = pltpu.get_barrier_semaphore()
    partners = [(level(k), t) for k in range(1, 4)] + [(d, tile(k)) for k in (-2, -1, 1, 2)]
    for partner in partners:
        pl.semaphore_signal(barrier, inc=1, device_id=partner, device_id_type=MESH)
    pl.semaphore_wait(barrier, len(partners))

    infos = [
        remote(positions, pos1, info_send.at[0], info_recv.at[0], (d, tile(1))),
        remote(positions, pos2, info_send.at[1], info_recv.at[1], (d, tile(2))),
        remote(occupied, occ2, info_send.at[2], info_recv.at[2], (d, tile(2))),
    ]
    for copy in infos:
        copy.start()
    meas_far = remote(measured.at[d], meas, meas_send, meas_recv, (d, tile(2)))
    for copy in infos:
        copy.wait_recv()

    own_row, own_col = positions[0, d], positions[1, d]
    row = jnp.where(far_slot, pos2[0, d], own_row)
    col = jnp.where(far_slot, pos2[1, d], own_col)
    weight = jnp.where(far_slot, occ2[d], occupied[d]).astype(F32)
    loads[0].wait()
    line = lax.broadcasted_iota(jnp.int32, (N, N), 0)
    lane = lax.broadcasted_iota(jnp.int32, (N, N), 1)
    turn_rows = (lax.bitwise_and(line - lane - row, N - 1) == 0).astype(F32).astype(BF)
    turn_cols = (lax.bitwise_and(lane - line - col, N - 1) == 0).astype(F32).astype(BF)
    for c in range(2):
        turned = exact_dot(lambda x: dot(turn_rows, x), wave0[c])
        psi[0, c] = exact_dot(lambda x: dot(x, turn_cols), turned)

    lax.fori_loop(0, blocks, lambda b, _: (block_load(b).wait(), 0)[1], 0)

    def cut_top(k):
        def store(c, rows, cols, x):
            mine[k, c, rows, cols] = x

        cut(spec, positions[0, k] - t * N, positions[1, k], True, store)

    def far_copy(k):
        return remote(mine.at[k], mine.at[k + 2], far_send.at[k - 2], far_recv.at[k - 2], (d, tile(2)))

    def halo_copy(k):
        to = jnp.where((odd == 1) | (k < 2), tile(-1), tile(1))
        return remote(halo_out.at[k], halo_in.at[k], halo_send.at[k], halo_recv.at[k], (d, to))

    @pl.when(odd == 1)
    def _():
        def body(k, _):
            cut_top(k)
            far_copy(k).start()
            return 0

        lax.fori_loop(2, 4, body, 0)

    @pl.when(far_slot)
    def _():
        meas_far.start()

    def cut_bottom(k, _):
        def store(c, rows, cols, x):
            halo_out[k, c, rows, cols] = x

        cut(spec, pos1[0, k] - tile(-1) * N, pos1[1, k], False, store)
        halo_copy(k).start()
        return 0

    lax.fori_loop(0, 4, cut_bottom, 0)

    def cut_mine(k, _):
        cut_top(k)
        return 0

    lax.fori_loop(0, jnp.where(odd == 1, 2, 4), cut_mine, 0)

    def y_copy(k):
        return remote(merged.at[k], waves.at[d], y_send.at[k], y_recv.at[d], (k, t))

    def merge(k, dst):
        halo_copy(k).wait_recv()

        @pl.when((odd == 1) & (k >= 2))
        def _():
            far_copy(k).wait_recv()

        source = jnp.where((odd == 1) & (k >= 2), k + 2, k)

        def body(i, _):
            rows = pl.ds(pl.multiple_of(i * 32, 32), 32)
            for c in range(2):
                dst[c, rows, :] = mine[source, c, rows, :] + halo_in[k, c, rows, :]
            return 0

        lax.fori_loop(0, N // 32, body, 0)

    for j in (1, 3, 2):
        k = level(j)
        merge(k, merged.at[k])
        y_copy(k).start()
    merge(d, waves.at[d])

    def arrived(s):
        @pl.when(s != d)
        def _():
            remote(merged.at[0], waves.at[s], y_send.at[0], y_recv.at[s], (s, t)).wait_recv()

    loads[1].wait()

    @pl.when(jnp.logical_not(far_slot))
    def _():
        meas_load.wait()

    @pl.when(far_slot)
    def _():
        meas_far.wait_recv()

    high, low = split(meas[...])
    high, low = split(dot(perm[...], high) + dot(perm[...], low))
    across = (((1,), (1,)), ((), ()))
    mp[...] = lax.dot_general(high, perm[...], across, preferred_element_type=F32) + lax.dot_general(
        low, perm[...], across, preferred_element_type=F32
    )
    loads[2].wait()

    def through(s, vr, vi):
        tr, ti = waves[s, 0], waves[s, 1]
        butterfly_store(tr * vr - ti * vi, tr * vi + ti * vr, dbuf)

    def forward(s, _):
        arrived(s)
        through(s, psi[s, 0], psi[s, 1])
        left_product(0, tab, dbuf, ebuf)
        o = unbutterfly(right_product(0, tab, ebuf))
        psi[s + 1, 0] = o[0]
        psi[s + 1, 1] = o[1]
        return 0

    lax.fori_loop(0, 3, forward, 0)
    arrived(3)
    through(3, psi[3, 0], psi[3, 1])
    left_product(1, tab, dbuf, ebuf)
    far = right_product(1, tab, ebuf)
    for b in range(2):
        fr, fi = far[b][:, :H], far[b][:, H:]
        excess = fr * fr + fi * fi - mp[:, half(b)]
        for c, z in ((0, excess * fr), (1, -(excess * fi))):
            for a in range(2):
                put(dbuf, a, half(c), half(b), z[half(a)])
    left_product(2, tab, dbuf, ebuf)
    o = unbutterfly(right_product(2, tab, ebuf))
    g[0] = o[0]
    g[1] = o[1]

    def g_copy(s):
        return remote(grads.at[s], grads_in.at[d], g_send.at[s], g_recv.at[d], (s, t))

    def contribute(s):
        pr, pi = psi[s, 0], psi[s, 1]
        gr, gi = g[0], g[1]
        grads[s, 0] = weight * (pr * gr - pi * gi)
        grads[s, 1] = -weight * (pr * gi + pi * gr)

        @pl.when(s != d)
        def _():
            g_copy(s).start()

    def backward(i, _):
        s = 3 - i
        contribute(s)
        through(s, g[0], g[1])
        left_product(0, tab, dbuf, ebuf)
        o = unbutterfly(right_product(0, tab, ebuf))
        g[0] = o[0]
        g[1] = o[1]
        return 0

    lax.fori_loop(0, 3, backward, 0)
    contribute(0)

    def spill_copy(src, k):
        to = jnp.where((odd == 1) & (k >= 2), tile(-1), tile(1))
        return remote(src, spill_out.at[k], spill_send.at[k], spill_recv.at[k], (d, to))

    def back_copy(src, k):
        return remote(src, own_out.at[k], back_send.at[k - 2], back_recv.at[k - 2], (d, tile(-2)))

    def own_copy(src, k):
        return pltpu.make_async_copy(src, own_out.at[k], out_sem.at[k])

    def place(src, k):
        spill_copy(src, k).start()

        @pl.when((odd == 1) & (k >= 2))
        def _():
            back_copy(src, k).start()

        @pl.when((odd == 0) | (k < 2))
        def _():
            own_copy(src, k).start()

    place(grads.at[d], d)
    for j in (1, 3, 2):
        k = level(j)
        remote(grads.at[0], grads_in.at[k], g_send.at[0], g_recv.at[k], (k, t)).wait_recv()
        place(grads_in.at[k], k)

    for r in range(2):
        for k in range(4):
            before_out[r, k] = pos1[r, k]

    for copy in infos:
        copy.wait_send()

    @pl.when(far_slot)
    def _():
        meas_far.wait_send()

    for k in range(4):
        halo_copy(k).wait_send()
        spill_copy(grads.at[0], k).wait()

        @pl.when(k != d)
        def _():
            y_copy(k).wait_send()
            g_copy(k).wait_send()

        if k < 2:
            own_copy(grads.at[0], k).wait()
        else:

            @pl.when(odd == 1)
            def _():
                far_copy(k).wait_send()
                back_copy(grads.at[0], k).wait()

            @pl.when(odd == 0)
            def _():
                own_copy(grads.at[0], k).wait()


def place_pieces(tiles, own, spill, positions, before, out, canvas, pieces, in_sem, out_sem):
    t = lax.axis_index("tile")
    loads = [pltpu.make_async_copy(own.at[k], pieces.at[k], in_sem.at[k]) for k in range(4)]
    loads += [pltpu.make_async_copy(spill.at[k], pieces.at[4 + k], in_sem.at[4 + k]) for k in range(4)]
    for copy in loads:
        copy.start()

    def clear(i, _):
        rows = pl.ds(pl.multiple_of(i * 8, 8), 8)
        for c in range(2):
            canvas[c, rows, :] = jnp.zeros((8, canvas.shape[2]), F32)
        return 0

    lax.fori_loop(0, N // 8, clear, 0)

    def add(k, row, col, top):
        block = lax.shift_right_logical(col, 7)
        rem = lax.bitwise_and(col, 127)
        odd = lax.bitwise_and(block, 1)
        chunk = 32

        def body(i, _):
            rows = pl.ds(pl.multiple_of(i * chunk, chunk), chunk)
            lane = lax.broadcasted_iota(jnp.int32, (chunk, H), 1)
            line = lax.broadcasted_iota(jnp.int32, (chunk, H), 0) + i * chunk
            keep = line >= row if top else line < row
            for c in range(2):
                same = pieces[k, c, rows, pl.ds(pl.multiple_of(odd * H, H), H)]
                other = pieces[k, c, rows, pl.ds(pl.multiple_of((1 - odd) * H, H), H)]
                for n, mask, x in ((0, keep & (lane >= rem), same), (1, keep, other), (2, keep & (lane < rem), same)):
                    cols = pl.ds(pl.multiple_of(jnp.minimum(block + n, 31) * H, H), H)
                    canvas[c, rows, cols] += jnp.where(mask, x, 0.0)
            return 0

        lax.fori_loop(0, N // chunk, body, 0)

    for k in range(4):
        loads[k].wait()
        add(k, positions[0, k] - t * N, positions[1, k], True)
    for k in range(4):
        loads[4 + k].wait()
        add(4 + k, before[0, k] - lax.rem(t + tiles - 1, tiles) * N, before[1, k], False)
    copy = pltpu.make_async_copy(canvas, out.at[:, 0], out_sem)
    copy.start()
    copy.wait()


def solution(mesh):
    depth, tiles = mesh.shape["depth"], mesh.shape["tile"]
    tables, order = transform_tables(), order_table()
    hbm = pl.BlockSpec(memory_space=pl.ANY)
    smem = pl.BlockSpec(memory_space=pltpu.SMEM)
    dma = pltpu.SemaphoreType.DMA

    def local(specimen, positions, occupied, measured, probe_wave):
        columns = specimen.shape[-1]
        own, spill, before = pl.pallas_call(
            functools.partial(gradient_pieces, depth, tiles),
            out_shape=(
                jax.ShapeDtypeStruct((4, *PIECE), F32),
                jax.ShapeDtypeStruct((4, *PIECE), F32),
                jax.ShapeDtypeStruct((2, 4), jnp.int32),
            ),
            in_specs=[hbm, smem, smem, hbm, hbm, hbm, hbm],
            out_specs=(hbm, hbm, smem),
            scratch_shapes=[
                pltpu.VMEM((columns // H, 2, N, H), F32),
                pltpu.VMEM((6, *PIECE), F32),
                pltpu.VMEM((4, *PIECE), F32),
                pltpu.VMEM((4, *PIECE), F32),
                pltpu.VMEM((4, *PIECE), F32),
                pltpu.VMEM((4, *PIECE), F32),
                pltpu.VMEM((4, *PIECE), F32),
                pltpu.VMEM(PIECE, F32),
                pltpu.VMEM((2, 2, N, N), BF),
                pltpu.VMEM((2, 2, N, N), BF),
                pltpu.VMEM((4, *PIECE), F32),
                pltpu.VMEM((4, *PIECE), F32),
                pltpu.VMEM(tables.shape, BF),
                pltpu.VMEM(order.shape, BF),
                pltpu.VMEM((N, N), F32),
                pltpu.VMEM((N, N), F32),
                pltpu.VMEM(PIECE, F32),
                pltpu.SMEM((2, 4), jnp.int32),
                pltpu.SMEM((2, 4), jnp.int32),
                pltpu.SMEM((4,), jnp.int32),
                dma((4,)), dma((columns // H,)), dma((3,)), dma((3,)), dma((4,)), dma((4,)), dma((2,)), dma((2,)),
                dma((4,)), dma((4,)), dma((4,)), dma((4,)), dma((4,)), dma((4,)), dma((2,)), dma((2,)),
                dma(()), dma(()), dma((4,)),
            ],
            compiler_params=pltpu.CompilerParams(
                collective_id=0, has_side_effects=True, vmem_limit_bytes=56 * 2**20
            ),
        )(specimen, positions, occupied, measured, probe_wave, tables, order)
        return pl.pallas_call(
            functools.partial(place_pieces, tiles),
            out_shape=jax.ShapeDtypeStruct(specimen.shape, F32),
            in_specs=[hbm, hbm, smem, smem],
            out_specs=hbm,
            scratch_shapes=[
                pltpu.VMEM((2, N, columns), F32),
                pltpu.VMEM((8, *PIECE), F32),
                dma((8,)),
                dma(()),
            ],
            compiler_params=pltpu.CompilerParams(vmem_limit_bytes=32 * 2**20),
        )(own, spill, positions, before)

    return jax.shard_map(
        local,
        mesh=mesh,
        in_specs=(P(None, "depth", "tile", None), P(None, "tile"), P("tile"), P("tile", None, None), P()),
        out_specs=P(None, "depth", "tile", None),
        check_vma=False,
    )
```

time: 796 us -> 96.6 us (0.12)
  waiting for transfers between devices: 428 us -> 0 us
  starting transfers between devices: 128 us -> 0 us
  Pallas kernels: 0 us -> 91.6 us
  local copies, waits for them, and re-layouts: 89.7 us -> 3.84 us
  loops' own time: 75.4 us -> 0 us
  other arithmetic: 46.4 us -> 0 us
  matrix products: 19.3 us -> 0 us
    ppermute x8 -> x0, waiting for transfers between devices: 428 us -> none  [from_behind(): lax.ppermute(value, axis, [(source, source + steps) for source in range(f...]
    ppermute x8 -> x0, starting transfers between devices: 128 us -> none  [from_behind(): lax.ppermute(value, axis, [(source, source + steps) for source in range(f...]
    pallas_call x0 -> x2, Pallas kernels: none -> 91.6 us  [the longest x1 84.6 us: local(): pl.pallas_call(functools.partial(gradient_pieces, depth, tiles), out_shap...]
    another operation x12 -> x0, loops' own time: 75.4 us -> none  [the longest x4 30.9 us: local(): lax.cond(active & (depth_index == depth_count - 1), from_detector, from_b...]
    dynamic_update_slice x4 -> x0, local copies, waits for them, and re-layouts: 26.2 us -> none  [place_wide(): lax.dynamic_update_slice(canvas, existing + patch_grads[slot_number], ind...]
    dot_general x12 -> x0, matrix products: 19.3 us -> none  [product(): return jnp.matmul(left_side, right_side, precision=PRECISE)]
    gather x12 -> x0, local copies, waits for them, and re-layouts: 16.3 us -> none
    another operation x8 -> x0, local copies, waits for them, and re-layouts: 12.1 us -> none
  transfers between devices with their start and end apart: 8 -> 0, of which waited for: 8 -> 0; matrix products, arithmetic and copies ran while one was open for 2% -> 0% of each run, Pallas kernels for 0% -> 0%
where the time goes in v1:
time: 96.6 us; the launch traced here: 95.4 us
  Pallas kernels  91.6 us (95%)
  local copies, waits for them, and re-layouts  3.84 us (4%)
    pallas_call x1, Pallas kernels, local(): pl.pallas_call(functools.partial(gradient_pieces, depth, tiles), out_shap...  84.6 us
    pallas_call x1, Pallas kernels, local(): pl.pallas_call(functools.partial(place_pieces, tiles), out_shape=jax.Shap...  7 us
    unnamed x8, local copies, waits for them, and re-layouts  3.84 us

profile of v1, /device:TPU:1, one launch (start us, length us, event | category | flops | bytes accessed | tf_op | source)
XLA Modules:
  0.0 95.4 jit_solution(63143716697413663)
XLA Ops:
  0.0 0.0 copy-start.2
  0.0 84.6 %shard_map.73 = (f32[4,2,256,256]{3,2,1,0:T(8,128)}, f32[4,2,256,256]{3,2,1,0:T(8,128)}, s32[2,4]{1,0:T(2,128)}) custom-call(f32[2,1,256,4096]{3,2,1,0:T(8,128)} %specimen.1, s32[2,4]{1,0:T(2,128)} %positions.3, s32[4]{0:T(128)} %occupied.1, f32[4,256,256]{2,1,0:T(8,128)} %measured.1, f32[2,256,256]{2,1,0:T(8,128)} %probe.1, ...), custom_call_target="tpu_custom_call" | custom-call | tf_op jit(solution)/shard_map/pallas_call | solution.py:475
  84.6 0.0 copy-done.2
  84.6 0.0 copy-start
  84.6 1.6 %copy-done = f32[4,2,256,256]{3,2,1,0:T(8,128)S(1)} copy-done((f32[4,2,256,256]{3,2,1,0:T(8,128)S(1)}, f32[4,2,256,256]{3,2,1,0:T(8,128)}, u32[]{:S(2)}) %copy-start) | copy-done | bytes 2097176
  86.2 0.0 copy-start.1
  86.2 1.6 %copy-done.1 = f32[4,2,256,256]{3,2,1,0:T(8,128)S(1)} copy-done((f32[4,2,256,256]{3,2,1,0:T(8,128)S(1)}, f32[4,2,256,256]{3,2,1,0:T(8,128)}, u32[]{:S(2)}) %copy-start.1) | copy-done | bytes 2097176
  87.8 0.0 copy-start.3
  87.8 0.7 copy-done.3
  88.4 7.0 %shard_map.74 = f32[2,1,256,4096]{3,2,1,0:T(8,128)} custom-call(f32[4,2,256,256]{3,2,1,0:T(8,128)S(1)} %copy-done, f32[4,2,256,256]{3,2,1,0:T(8,128)S(1)} %copy-done.1, s32[2,4]{1,0:T(2,128)S(1)} %copy-done.2, s32[2,4]{1,0:T(2,128)S(1)} %copy-done.3), custom_call_target="tpu_custom_call" | custom-call | tf_op jit(solution)/shard_map/pallas_call | solution.py:513
Async XLA Ops:
  0.0 84.6 %copy-start.2 = (s32[2,4]{1,0:T(2,128)S(1)}, s32[2,4]{1,0:T(2,128)}, u32[]{:S(2)}) copy-start(s32[2,4]{1,0:T(2,128)} %positions.3) | copy-start | bytes 100
  84.6 1.6 %copy-start = (f32[4,2,256,256]{3,2,1,0:T(8,128)S(1)}, f32[4,2,256,256]{3,2,1,0:T(8,128)}, u32[]{:S(2)}) copy-start(f32[4,2,256,256]{3,2,1,0:T(8,128)} %get-tuple-element.8.own) | copy-start | bytes 6291460
  86.2 1.6 %copy-start.1 = (f32[4,2,256,256]{3,2,1,0:T(8,128)S(1)}, f32[4,2,256,256]{3,2,1,0:T(8,128)}, u32[]{:S(2)}) copy-start(f32[4,2,256,256]{3,2,1,0:T(8,128)} %get-tuple-element.9.spill) | copy-start | bytes 6291460
  87.8 0.7 copy-start.3

commit v2 on v1

v2 whole, which is shorter than its diff:
```python
import functools
import math

import jax
import jax.numpy as jnp
import ml_dtypes
import numpy as np
from jax import lax
from jax.experimental import pallas as pl
from jax.experimental.pallas import tpu as pltpu
from jax.sharding import PartitionSpec as P

MESH = pl.DeviceIdType.MESH
BF = jnp.bfloat16
F32 = jnp.float32
N = 256
H = 128
PIECE = (2, N, N)


def transform_tables():
    j = np.arange(N)
    unitary = np.exp(-2j * np.pi * ((j[:, None] * j[None, :]) % N) / N) / math.sqrt(N)
    f = ((j + H) % N) - H
    kernel = np.conj(unitary) @ (np.exp(-12j * f * f / (N * N))[:, None] * unitary)
    kernels = [(kernel[:H, :H] + sign * kernel[:H, H:]) / 2 for sign in (1, -1)]
    halves = [unitary[:H, 0::2], unitary[:H, 1::2]]

    def left(m):
        return np.block([[m.real, -m.imag], [m.imag, m.real]])

    def right(m):
        return np.block([[m.real, m.imag], [-m.imag, m.real]])

    lefts = [[left(m) for m in kernels], [left(m.T) for m in halves], [left(m) for m in halves]]
    rights = [[right(m) for m in kernels], [right(m) for m in halves], [right(m.T) for m in halves]]
    exact = np.array([lefts, rights])
    high = exact.astype(ml_dtypes.bfloat16)
    low = (exact - high.astype(np.float64)).astype(ml_dtypes.bfloat16)
    return np.stack([high, low], axis=3)


def order_table():
    table = np.zeros((N, N))
    table[np.arange(N), np.r_[0:N:2, 1:N:2]] = 1
    return table.astype(ml_dtypes.bfloat16)


def split(x):
    high = x.astype(BF)
    return high, (x - high.astype(F32)).astype(BF)


def dot(a, b):
    return jnp.dot(a, b, preferred_element_type=F32)


def exact_dot(multiply, x):
    high = x.astype(BF)
    rest = x - high.astype(F32)
    middle = rest.astype(BF)
    low = (rest - middle.astype(F32)).astype(BF)
    return multiply(high) + (multiply(middle) + multiply(low))


def put(buf, index, rows, cols, x):
    high, low = split(x)
    buf[index, 0, rows, cols] = high
    buf[index, 1, rows, cols] = low


def half(i):
    return slice(i * H, (i + 1) * H)


def butterfly_store(xr, xi, dbuf):
    for c, x in ((0, xr), (1, xi)):
        top, bottom = x[:H], x[H:]
        for a, y in ((0, top + bottom), (1, top - bottom)):
            put(dbuf, a, half(c), half(0), y[:, :H] + y[:, H:])
            put(dbuf, a, half(c), half(1), y[:, :H] - y[:, H:])


def left_product(kind, tab, dbuf, ebuf):
    for a in range(2):
        high, low = dbuf[a, 0], dbuf[a, 1]
        e = dot(tab[0, kind, a, 0], high) + (dot(tab[0, kind, a, 0], low) + dot(tab[0, kind, a, 1], high))
        for c in range(2):
            for b in range(2):
                put(ebuf, b, half(a), half(c), e[half(c), half(b)])


def right_product(kind, tab, ebuf):
    out = []
    for b in range(2):
        high, low = ebuf[b, 0], ebuf[b, 1]
        out.append(dot(high, tab[1, kind, b, 0]) + (dot(low, tab[1, kind, b, 0]) + dot(high, tab[1, kind, b, 1])))
    return out


def unbutterfly(g):
    res = []
    for c in range(2):
        p, m = g[0][:, half(c)], g[1][:, half(c)]
        y = jnp.concatenate([p + m, p - m], axis=1)
        res.append(jnp.concatenate([y[:H] + y[H:], y[:H] - y[H:]], axis=0))
    return res


def cut(spec, row, col, top, store):
    block = lax.div(col, H)
    rem = lax.rem(col, H)
    odd = lax.rem(block, 2)
    chunk = 32

    def body(i, _):
        rows = pl.ds(pl.multiple_of(i * chunk, chunk), chunk)
        lane = lax.broadcasted_iota(jnp.int32, (chunk, H), 1)
        line = lax.broadcasted_iota(jnp.int32, (chunk, H), 0) + i * chunk
        keep = line >= row if top else line < row
        for side in range(2):
            first = block + (odd if side == 0 else 1 - odd)
            second = first + 2 - 2 * lax.div(first + 2, 32)
            limit = rem * (1 - odd if side == 0 else odd)
            for c in range(2):
                here = spec[first, c, rows, :]
                there = spec[second, c, rows, :]
                store(c, rows, half(side), jnp.where(keep, jnp.where(lane >= limit, here, there), 0.0))
        return 0

    lax.fori_loop(0, N // chunk, body, 0)


def add_pieces(canvas, pool, pieces):
    chunk = 16

    def body(i, _):
        rows = pl.ds(pl.multiple_of(i * chunk, chunk), chunk)
        lane = lax.broadcasted_iota(jnp.int32, (chunk, H), 1)
        line = lax.broadcasted_iota(jnp.int32, (chunk, H), 0) + i * chunk
        keeps = [line >= row if top else line < row for _, row, _, top in pieces]
        for c in range(2):
            values = [
                [jnp.where(keep, pool[slot, c, rows, half(h)], 0.0) for h in range(2)]
                for keep, (slot, _, _, _) in zip(keeps, pieces)
            ]
            for b in range(canvas.shape[2] // H):
                total = canvas[c, rows, half(b)]
                for value, (_, _, col, _) in zip(values, pieces):
                    at = lane + (b * H - col)
                    total += jnp.where((at >= 0) & (at < N), value[b % 2], 0.0)
                canvas[c, rows, half(b)] = total
        return 0

    lax.fori_loop(0, N // chunk, body, 0)


def gradient_kernel(
    depth, tiles, specimen, positions, occupied, measured, probe, tables, order, canvas,
    spec, mine, halo_out, halo_in, merged, waves, psi, g, dbuf, ebuf, pool, tab, perm, meas, mp,
    wave0, pos0, pos1, pos2,
    load_sem, spec_sem, info_send, info_recv, halo_send, halo_recv, far_send, far_recv, y_send, y_recv,
    g_send, g_recv, spill_send, spill_recv, back_send, back_recv, meas_send, meas_recv, turn_sem,
):
    d = lax.axis_index("depth")
    t = lax.axis_index("tile")
    odd = lax.rem(t, 2)
    both = range(2)

    def tile(k):
        return lax.rem(t + k + tiles, tiles)

    def level(k):
        return lax.rem(d + k, depth)

    def remote(src, dst, send, recv, to):
        return pltpu.make_async_remote_copy(
            src_ref=src, dst_ref=dst, send_sem=send, recv_sem=recv, device_id=to, device_id_type=MESH
        )

    near = lax.rem(d + 1, 2)
    turns = (near, near + 2, level(2), d)
    far_slot = (odd == 1) & (d >= 2)

    probe_load = pltpu.make_async_copy(probe, wave0, load_sem.at[0])
    order_load = pltpu.make_async_copy(order, perm, load_sem.at[1])
    tables_load = pltpu.make_async_copy(tables, tab, load_sem.at[2])
    meas_load = pltpu.make_async_copy(measured.at[d], meas, load_sem.at[3])
    blocks = spec.shape[0]

    def block_load(b):
        cols = pl.ds(pl.multiple_of(b * H, H), H)
        return pltpu.make_async_copy(specimen.at[:, 0, :, cols], spec.at[b], spec_sem.at[b])

    lax.fori_loop(0, blocks, lambda b, _: (block_load(b).start(), 0)[1], 0)
    probe_load.start()
    order_load.start()

    @pl.when(jnp.logical_not(far_slot))
    def _():
        meas_load.start()

    tables_load.start()

    barrier = pltpu.get_barrier_semaphore()
    partners = [(level(k), t) for k in range(1, 4)] + [(d, tile(k)) for k in (-1, 1)]
    wide = [(d, tile(k)) for k in (-2, 2)]
    for partner in partners:
        pl.semaphore_signal(barrier, inc=1, device_id=partner, device_id_type=MESH)

    @pl.when(odd == 1)
    def _():
        for partner in wide:
            pl.semaphore_signal(barrier, inc=1, device_id=partner, device_id_type=MESH)

    for k in range(4):
        pos0[0, k] = (positions[0, k] - t * N) * occupied[k]
        pos0[1, k] = positions[1, k]

    def cut_top(k):
        def store(c, rows, cols, x):
            mine[k, c, rows, cols] = x

        cut(spec, pos0[0, k] + N * (1 - occupied[k]), pos0[1, k], True, store)

    def turn_probe(row, col):
        line = lax.broadcasted_iota(jnp.int32, (N, N), 0)
        lane = lax.broadcasted_iota(jnp.int32, (N, N), 1)
        turn_rows = (lax.bitwise_and(line - lane - row, N - 1) == 0).astype(F32).astype(BF)
        turn_cols = (lax.bitwise_and(lane - line - col, N - 1) == 0).astype(F32).astype(BF)
        for c in both:
            turned = exact_dot(lambda x: dot(turn_rows, x), wave0[c])
            psi[0, c] = exact_dot(lambda x: dot(x, turn_cols), turned)

    def order_measured():
        high, low = split(meas[...])
        high, low = split(dot(perm[...], high) + dot(perm[...], low))
        across = (((1,), (1,)), ((), ()))
        mp[...] = lax.dot_general(high, perm[...], across, preferred_element_type=F32) + lax.dot_general(
            low, perm[...], across, preferred_element_type=F32
        )

    def clear(i, _):
        rows = pl.ds(pl.multiple_of(i * 8, 8), 8)
        for c in both:
            canvas[c, rows, :] = jnp.zeros((8, canvas.shape[2]), F32)
        return 0

    pl.semaphore_wait(barrier, jnp.where(odd == 1, len(partners) + len(wide), len(partners)))

    info1 = remote(pos0, pos1, info_send.at[0], info_recv.at[0], (d, tile(1)))
    info2 = remote(pos0, pos2, info_send.at[1], info_recv.at[1], (d, tile(2)))
    meas_far = remote(measured.at[d], meas, meas_send, meas_recv, (d, tile(2)))

    def far_copy(k, c):
        return remote(mine.at[k, c], mine.at[k + 2, c], far_send.at[k - 2, c], far_recv.at[k - 2, c], (d, tile(2)))

    def halo_copy(k, c):
        to = jnp.where((odd == 1) | (k < 2), tile(-1), tile(1))
        return remote(halo_out.at[k, c], halo_in.at[k, c], halo_send.at[k, c], halo_recv.at[k, c], (d, to))

    info1.start()

    @pl.when(odd == 1)
    def _():
        info2.start()

    lax.fori_loop(0, blocks, lambda b, _: (block_load(b).wait(), 0)[1], 0)

    @pl.when(odd == 1)
    def _():
        for k in (near + 2, 3 - near):
            cut_top(k)
            for c in both:
                far_copy(k, c).start()

    @pl.when(far_slot)
    def _():
        meas_far.start()

    info1.wait_recv()

    def cut_bottom(k):
        def store(c, rows, cols, x):
            halo_out[k, c, rows, cols] = x

        cut(spec, pos1[0, k], pos1[1, k], False, store)
        for c in both:
            halo_copy(k, c).start()

    for k in turns:
        cut_bottom(k)
    for k in turns:

        @pl.when((odd == 0) | (k < 2))
        def _():
            cut_top(k)

    def y_copy(k, c):
        return remote(merged.at[k, c], waves.at[d, c], y_send.at[k, c], y_recv.at[d, c], (k, t))

    def merge(k, c, dst):
        halo_copy(k, c).wait_recv()

        @pl.when((odd == 1) & (k >= 2))
        def _():
            far_copy(k, c).wait_recv()

        source = jnp.where((odd == 1) & (k >= 2), k + 2, k)

        def body(i, _):
            rows = pl.ds(pl.multiple_of(i * 64, 64), 64)
            dst[c, rows, :] = mine[source, c, rows, :] + halo_in[k, c, rows, :]
            return 0

        lax.fori_loop(0, N // 64, body, 0)

    def merge_level(k):
        for c in both:
            merge(k, c, merged.at[k])

    def send_level(k):
        for c in both:
            y_copy(k, c).start()

    merge_level(turns[0])
    merge_level(turns[1])

    @pl.when(odd == 0)
    def _():
        send_level(turns[0])
        send_level(turns[1])
        merge_level(turns[2])
        send_level(turns[2])

    @pl.when(odd == 1)
    def _():
        info2.wait_recv()

    probe_load.wait()
    turn_probe(jnp.where(far_slot, pos2[0, d], pos0[0, d]), jnp.where(far_slot, pos2[1, d], pos0[1, d]))
    lax.fori_loop(0, N // 8, clear, 0)

    @pl.when(odd == 1)
    def _():
        pl.semaphore_wait(turn_sem.at[0], 1)
        send_level(turns[0])
        send_level(turns[1])
        merge_level(turns[2])
        send_level(turns[2])

    for c in both:
        merge(d, c, waves.at[d])

    @pl.when(odd == 0)
    def _():
        for k in turns[:2]:
            for c in both:
                y_copy(k, c).wait_send()
        y_copy(turns[2], 0).wait_send()
        pl.semaphore_signal(turn_sem.at[0], inc=1, device_id=(d, t + 1), device_id_type=MESH)

    order_load.wait()

    @pl.when(far_slot)
    def _():
        meas_far.wait_recv()

    @pl.when(jnp.logical_not(far_slot))
    def _():
        meas_load.wait()

    order_measured()
    tables_load.wait()

    def arrived(s):
        @pl.when(s != d)
        def _():
            for c in both:
                remote(merged.at[0, c], waves.at[s, c], y_send.at[0, c], y_recv.at[s, c], (s, t)).wait_recv()

    def through(s, vr, vi):
        tr, ti = waves[s, 0], waves[s, 1]
        butterfly_store(tr * vr - ti * vi, tr * vi + ti * vr, dbuf)

    def forward(s, _):
        arrived(s)
        through(s, psi[s, 0], psi[s, 1])
        left_product(0, tab, dbuf, ebuf)
        o = unbutterfly(right_product(0, tab, ebuf))
        psi[s + 1, 0] = o[0]
        psi[s + 1, 1] = o[1]
        return 0

    lax.fori_loop(0, 3, forward, 0)
    arrived(3)

    through(3, psi[3, 0], psi[3, 1])
    left_product(1, tab, dbuf, ebuf)
    far = right_product(1, tab, ebuf)
    for b in both:
        fr, fi = far[b][:, :H], far[b][:, H:]
        excess = fr * fr + fi * fi - mp[:, half(b)]
        for c, z in ((0, excess * fr), (1, -(excess * fi))):
            for a in both:
                put(dbuf, a, half(c), half(b), z[half(a)])
    left_product(2, tab, dbuf, ebuf)
    o = unbutterfly(right_product(2, tab, ebuf))
    g[0] = o[0]
    g[1] = o[1]

    def g_copy(s, c):
        return remote(pool.at[s + 6, c], pool.at[d, c], g_send.at[s, c], g_recv.at[d, c], (s, t))

    def contribute(s):
        slot = jnp.where(s == d, d, s + 6)
        pr, pi = psi[s, 0], psi[s, 1]
        gr, gi = g[0], g[1]
        pool[slot, 0] = pr * gr - pi * gi
        pool[slot, 1] = -(pr * gi + pi * gr)

    def backward(i, _):
        s = 3 - i
        contribute(s)
        through(s, g[0], g[1])
        left_product(0, tab, dbuf, ebuf)
        o = unbutterfly(right_product(0, tab, ebuf))
        g[0] = o[0]
        g[1] = o[1]
        return 0

    lax.fori_loop(0, 3, backward, 0)
    contribute(0)

    def spill_copy(k, c):
        to = jnp.where((odd == 1) & (k >= 2), tile(-1), tile(1))
        return remote(pool.at[k, c], pool.at[k + 10, c], spill_send.at[k, c], spill_recv.at[k, c], (d, to))

    def back_copy(k, c):
        return remote(pool.at[k, c], pool.at[k + 2, c], back_send.at[k - 2, c], back_recv.at[k - 2, c], (d, tile(-2)))

    def send_back(k, c):
        g_copy(k, c).start()

    def pass_on(k):
        for c in both:

            @pl.when(k != d)
            def _():
                remote(pool.at[6, c], pool.at[k, c], g_send.at[0, c], g_recv.at[k, c], (k, t)).wait_recv()

            @pl.when((odd == 1) & (k >= 2))
            def _():
                back_copy(k, c).start()

            spill_copy(k, c).start()

    def mine_of(k):
        @pl.when((odd == 1) & (k >= 2))
        def _():
            for c in both:
                back_copy(k, c).wait_recv()

        return (jnp.where((odd == 1) & (k >= 2), k + 2, k), pos0[0, k], pos0[1, k], True)

    def spilled_of(k):
        for c in both:
            spill_copy(k, c).wait_recv()
        return (k + 10, pos1[0, k], pos1[1, k], False)

    first, second, across = turns[:3]

    @pl.when(odd == 0)
    def _():
        for c in both:
            send_back(first, c)
            send_back(second, c)
        send_back(across, 0)

    @pl.when(odd == 1)
    def _():
        for c in both:
            send_back(first, c)
            send_back(second, c)

    pass_on(d)

    @pl.when(odd == 1)
    def _():
        for c in both:
            g_copy(first, c).wait_send()
            g_copy(second, c).wait_send()
        for c in both:
            send_back(across, c)

    pass_on(first)
    pass_on(second)

    @pl.when(odd == 0)
    def _():
        add_pieces(canvas, pool, [mine_of(d)])
        add_pieces(canvas, pool, [mine_of(first), mine_of(second)])
        pl.semaphore_wait(turn_sem.at[1], 1)
        send_back(across, 1)
        add_pieces(canvas, pool, [spilled_of(d), spilled_of(first), spilled_of(second)])
        pass_on(across)

    @pl.when(odd == 1)
    def _():
        add_pieces(canvas, pool, [mine_of(d)])
        g_copy(across, 0).wait_send()
        pl.semaphore_signal(turn_sem.at[1], inc=1, device_id=(d, t - 1), device_id_type=MESH)
        add_pieces(canvas, pool, [spilled_of(d), spilled_of(first), spilled_of(second)])
        pass_on(across)
        add_pieces(canvas, pool, [mine_of(first), mine_of(second)])

    add_pieces(canvas, pool, [mine_of(across), spilled_of(across)])

    info1.wait_send()

    @pl.when(far_slot)
    def _():
        meas_far.wait_send()

    @pl.when(odd == 1)
    def _():
        info2.wait_send()
        for c in both:
            for k in (2, 3):
                far_copy(k, c).wait_send()
                back_copy(k, c).wait_send()
            y_copy(first, c).wait_send()
            y_copy(second, c).wait_send()
        y_copy(across, 0).wait_send()
        g_copy(across, 1).wait_send()

    @pl.when(odd == 0)
    def _():
        for c in both:
            for k in (first, second, across):
                g_copy(k, c).wait_send()

    y_copy(across, 1).wait_send()
    for k in range(4):
        for c in both:
            halo_copy(k, c).wait_send()
            spill_copy(k, c).wait_send()


def solution(mesh):
    depth, tiles = mesh.shape["depth"], mesh.shape["tile"]
    tables, order = transform_tables(), order_table()
    hbm = pl.BlockSpec(memory_space=pl.ANY)
    smem = pl.BlockSpec(memory_space=pltpu.SMEM)
    dma = pltpu.SemaphoreType.DMA

    def pieces(count):
        return pltpu.VMEM((count, *PIECE), F32)

    def local(specimen, positions, occupied, measured, probe_wave):
        columns = specimen.shape[-1]
        canvas = pl.pallas_call(
            functools.partial(gradient_kernel, depth, tiles),
            out_shape=pltpu.VMEM((2, N, columns), F32),
            in_specs=[hbm, smem, smem, hbm, hbm, hbm, hbm],
            out_specs=pl.BlockSpec(memory_space=pltpu.VMEM),
            scratch_shapes=[
                pltpu.VMEM((columns // H, 2, N, H), F32),
                pieces(6), pieces(4), pieces(4), pieces(4), pieces(4), pieces(4),
                pltpu.VMEM(PIECE, F32),
                pltpu.VMEM((2, 2, N, N), BF),
                pltpu.VMEM((2, 2, N, N), BF),
                pieces(14),
                pltpu.VMEM(tables.shape, BF),
                pltpu.VMEM(order.shape, BF),
                pltpu.VMEM((N, N), F32),
                pltpu.VMEM((N, N), F32),
                pltpu.VMEM(PIECE, F32),
                pltpu.SMEM((2, 4), jnp.int32),
                pltpu.SMEM((2, 4), jnp.int32),
                pltpu.SMEM((2, 4), jnp.int32),
                dma((4,)), dma((columns // H,)), dma((2,)), dma((2,)), dma((4, 2)), dma((4, 2)), dma((2, 2)), dma((2, 2)),
                dma((4, 2)), dma((4, 2)), dma((4, 2)), dma((4, 2)), dma((4, 2)), dma((4, 2)), dma((2, 2)), dma((2, 2)),
                dma(()), dma(()), pltpu.SemaphoreType.REGULAR((2,)),
            ],
            compiler_params=pltpu.CompilerParams(
                collective_id=0, has_side_effects=True, vmem_limit_bytes=48 * 2**20
            ),
        )(specimen, positions, occupied, measured, probe_wave, tables, order)
        return canvas[:, None]

    return jax.shard_map(
        local,
        mesh=mesh,
        in_specs=(P(None, "depth", "tile", None), P(None, "tile"), P("tile"), P("tile", None, None), P()),
        out_specs=P(None, "depth", "tile", None),
        check_vma=False,
    )
```

time: 96.6 us -> 73.7 us (0.76)
  Pallas kernels: 91.6 us -> 69 us
    pallas_call x2 -> x1, Pallas kernels: 91.6 us -> 69 us  [local(): pl.pallas_call(functools.partial(gradient_kernel, depth, tiles), out_shap...]
    unnamed x8 -> x1, local copies, waits for them, and re-layouts: 3.84 us -> 3.4 us
where the time goes in v2:
time: 73.7 us; the launch traced here: 72.4 us
  Pallas kernels  69 us (94%)
  local copies, waits for them, and re-layouts  3.4 us (5%)
    pallas_call x1, Pallas kernels, local(): pl.pallas_call(functools.partial(gradient_kernel, depth, tiles), out_shap...  69 us
    unnamed x1, local copies, waits for them, and re-layouts  3.4 us

profile of v2, /device:TPU:1, one launch (start us, length us, event | category | flops | bytes accessed | tf_op | source)
XLA Modules:
  0.0 72.4 jit_solution(8696271887396765193)
XLA Ops:
  0.0 69.0 %shard_map.73 = f32[2,256,4096]{2,1,0:T(8,128)S(1)} custom-call(f32[2,1,256,4096]{3,2,1,0:T(8,128)} %specimen.1, s32[2,4]{1,0:T(2,128)} %positions.1, s32[4]{0:T(128)} %occupied.1, f32[4,256,256]{2,1,0:T(8,128)} %measured.1, f32[2,256,256]{2,1,0:T(8,128)} %probe.1, bf16[2,3,2,2,256,256]{5,4,3,2,1,0:T(8,128)(2,1)} %constant.4.clone.tables, ...), custom_call_target="tpu_custom_call" | custom-call | tf_op jit(solution)/shard_map/pallas_call | solution.py:562
  69.0 3.4 %copy.10 = f32[2,1,256,4096]{3,2,1,0:T(8,128)} copy(f32[2,1,256,4096]{3,2,1,0:T(8,128)S(1)} %bitcast.3) | data formatting | bytes 16777216

commit v3 on v2

--- a/solution.py
+++ b/solution.py
@@ -131,7 +131,7 @@
     lax.fori_loop(0, N // chunk, body, 0)
 
 
-def add_pieces(canvas, pool, pieces):
+def add_pieces(canvas, pool, pieces, parts=(0, 1)):
     chunk = 16
 
     def body(i, _):
@@ -139,7 +139,7 @@
         lane = lax.broadcasted_iota(jnp.int32, (chunk, H), 1)
         line = lax.broadcasted_iota(jnp.int32, (chunk, H), 0) + i * chunk
         keeps = [line >= row if top else line < row for _, row, _, top in pieces]
-        for c in range(2):
+        for c in parts:
             values = [
                 [jnp.where(keep, pool[slot, c, rows, half(h)], 0.0) for h in range(2)]
                 for keep, (slot, _, _, _) in zip(keeps, pieces)
@@ -267,6 +267,24 @@
 
     lax.fori_loop(0, blocks, lambda b, _: (block_load(b).wait(), 0)[1], 0)
 
+    info1.wait_recv()
+
+    def cut_bottom(k):
+        def store(c, rows, cols, x):
+            halo_out[k, c, rows, cols] = x
+
+        cut(spec, pos1[0, k], pos1[1, k], False, store)
+        for c in both:
+            halo_copy(k, c).start()
+
+    def cut_mine(k):
+        @pl.when((odd == 0) | (k < 2))
+        def _():
+            cut_top(k)
+
+    cut_bottom(turns[0])
+    cut_bottom(turns[1])
+
     @pl.when(odd == 1)
     def _():
         for k in (near + 2, 3 - near):
@@ -278,23 +296,10 @@
     def _():
         meas_far.start()
 
-    info1.wait_recv()
-
-    def cut_bottom(k):
-        def store(c, rows, cols, x):
-            halo_out[k, c, rows, cols] = x
-
-        cut(spec, pos1[0, k], pos1[1, k], False, store)
-        for c in both:
-            halo_copy(k, c).start()
-
-    for k in turns:
-        cut_bottom(k)
-    for k in turns:
-
-        @pl.when((odd == 0) | (k < 2))
-        def _():
-            cut_top(k)
+    cut_bottom(turns[2])
+    cut_bottom(turns[3])
+    cut_mine(turns[0])
+    cut_mine(turns[1])
 
     def y_copy(k, c):
         return remote(merged.at[k, c], waves.at[d, c], y_send.at[k, c], y_recv.at[d, c], (k, t))
@@ -330,8 +335,15 @@
     def _():
         send_level(turns[0])
         send_level(turns[1])
+        cut_mine(turns[2])
         merge_level(turns[2])
         send_level(turns[2])
+        cut_mine(turns[3])
+
+    @pl.when(odd == 1)
+    def _():
+        cut_mine(turns[2])
+        cut_mine(turns[3])
 
     @pl.when(odd == 1)
     def _():
@@ -455,16 +467,16 @@
 
             spill_copy(k, c).start()
 
-    def mine_of(k):
+    def mine_of(k, parts=both):
         @pl.when((odd == 1) & (k >= 2))
         def _():
-            for c in both:
+            for c in parts:
                 back_copy(k, c).wait_recv()
 
         return (jnp.where((odd == 1) & (k >= 2), k + 2, k), pos0[0, k], pos0[1, k], True)
 
-    def spilled_of(k):
-        for c in both:
+    def spilled_of(k, parts=both):
+        for c in parts:
             spill_copy(k, c).wait_recv()
         return (k + 10, pos1[0, k], pos1[1, k], False)
 
@@ -514,7 +526,8 @@
         pass_on(across)
         add_pieces(canvas, pool, [mine_of(first), mine_of(second)])
 
-    add_pieces(canvas, pool, [mine_of(across), spilled_of(across)])
+    for c in both:
+        add_pieces(canvas, pool, [mine_of(across, (c,)), spilled_of(across, (c,))], (c,))
 
     info1.wait_send()
 

time: 73.7 us -> 72.2 us (0.980)
  Pallas kernels: 69 us -> 68.1 us
    pallas_call x1, Pallas kernels: 69 us -> 68.1 us  [local(): pl.pallas_call(functools.partial(gradient_kernel, depth, tiles), out_shap...]
where the time goes in v3:
time: 72.2 us; the launch traced here: 71.5 us
  Pallas kernels  68.1 us (94%)
  local copies, waits for them, and re-layouts  3.4 us (5%)
    pallas_call x1, Pallas kernels, local(): pl.pallas_call(functools.partial(gradient_kernel, depth, tiles), out_shap...  68.1 us
    unnamed x1, local copies, waits for them, and re-layouts  3.4 us

profile of v3, /device:TPU:1, one launch (start us, length us, event | category | flops | bytes accessed | tf_op | source)
XLA Modules:
  0.0 71.5 jit_solution(1600662679738573676)
XLA Ops:
  0.0 68.1 %shard_map.73 = f32[2,256,4096]{2,1,0:T(8,128)S(1)} custom-call(f32[2,1,256,4096]{3,2,1,0:T(8,128)} %specimen.1, s32[2,4]{1,0:T(2,128)} %positions.1, s32[4]{0:T(128)} %occupied.1, f32[4,256,256]{2,1,0:T(8,128)} %measured.1, f32[2,256,256]{2,1,0:T(8,128)} %probe.1, bf16[2,3,2,2,256,256]{5,4,3,2,1,0:T(8,128)(2,1)} %constant.4.clone.tables, ...), custom_call_target="tpu_custom_call" | custom-call | tf_op jit(solution)/shard_map/pallas_call | solution.py:575
  68.1 3.4 %copy.10 = f32[2,1,256,4096]{3,2,1,0:T(8,128)} copy(f32[2,1,256,4096]{3,2,1,0:T(8,128)S(1)} %bitcast.3) | data formatting | bytes 16777216

commit v4 on v3

--- a/solution.py
+++ b/solution.py
@@ -131,28 +131,29 @@
     lax.fori_loop(0, N // chunk, body, 0)
 
 
-def add_pieces(canvas, pool, pieces, parts=(0, 1)):
+def add_pieces(canvas, pool, pieces, parts=range(4)):
     chunk = 16
 
     def body(i, _):
         rows = pl.ds(pl.multiple_of(i * chunk, chunk), chunk)
         lane = lax.broadcasted_iota(jnp.int32, (chunk, H), 1)
-        line = lax.broadcasted_iota(jnp.int32, (chunk, H), 0) + i * chunk
-        keeps = [line >= row if top else line < row for _, row, _, top in pieces]
-        for c in parts:
+        for part in parts:
+            c, first = part // 2, part % 2 * H
+            line = lax.broadcasted_iota(jnp.int32, (chunk, H), 0) + (first + i * chunk)
+            here = pl.ds(pl.multiple_of(first + i * chunk, chunk), chunk)
             values = [
-                [jnp.where(keep, pool[slot, c, rows, half(h)], 0.0) for h in range(2)]
-                for keep, (slot, _, _, _) in zip(keeps, pieces)
+                [jnp.where(line >= row if top else line < row, pool[slot, part, rows, half(h)], 0.0) for h in range(2)]
+                for slot, row, _, top in pieces
             ]
             for b in range(canvas.shape[2] // H):
-                total = canvas[c, rows, half(b)]
+                total = canvas[c, here, half(b)]
                 for value, (_, _, col, _) in zip(values, pieces):
                     at = lane + (b * H - col)
                     total += jnp.where((at >= 0) & (at < N), value[b % 2], 0.0)
-                canvas[c, rows, half(b)] = total
+                canvas[c, here, half(b)] = total
         return 0
 
-    lax.fori_loop(0, N // chunk, body, 0)
+    lax.fori_loop(0, H // chunk, body, 0)
 
 
 def gradient_kernel(
@@ -166,6 +167,7 @@
     t = lax.axis_index("tile")
     odd = lax.rem(t, 2)
     both = range(2)
+    parts = range(4)
 
     def tile(k):
         return lax.rem(t + k + tiles, tiles)
@@ -193,15 +195,6 @@
         return pltpu.make_async_copy(specimen.at[:, 0, :, cols], spec.at[b], spec_sem.at[b])
 
     lax.fori_loop(0, blocks, lambda b, _: (block_load(b).start(), 0)[1], 0)
-    probe_load.start()
-    order_load.start()
-
-    @pl.when(jnp.logical_not(far_slot))
-    def _():
-        meas_load.start()
-
-    tables_load.start()
-
     barrier = pltpu.get_barrier_semaphore()
     partners = [(level(k), t) for k in range(1, 4)] + [(d, tile(k)) for k in (-1, 1)]
     wide = [(d, tile(k)) for k in (-2, 2)]
@@ -266,6 +259,14 @@
         info2.start()
 
     lax.fori_loop(0, blocks, lambda b, _: (block_load(b).wait(), 0)[1], 0)
+    probe_load.start()
+    order_load.start()
+
+    @pl.when(jnp.logical_not(far_slot))
+    def _():
+        meas_load.start()
+
+    tables_load.start()
 
     info1.wait_recv()
 
@@ -428,8 +429,9 @@
         slot = jnp.where(s == d, d, s + 6)
         pr, pi = psi[s, 0], psi[s, 1]
         gr, gi = g[0], g[1]
-        pool[slot, 0] = pr * gr - pi * gi
-        pool[slot, 1] = -(pr * gi + pi * gr)
+        for c, x in ((0, pr * gr - pi * gi), (1, -(pr * gi + pi * gr))):
+            pool[slot, 2 * c] = x[:H]
+            pool[slot, 2 * c + 1] = x[H:]
 
     def backward(i, _):
         s = 3 - i
@@ -455,7 +457,7 @@
         g_copy(k, c).start()
 
     def pass_on(k):
-        for c in both:
+        for c in parts:
 
             @pl.when(k != d)
             def _():
@@ -467,7 +469,7 @@
 
             spill_copy(k, c).start()
 
-    def mine_of(k, parts=both):
+    def mine_of(k, parts=range(4)):
         @pl.when((odd == 1) & (k >= 2))
         def _():
             for c in parts:
@@ -475,7 +477,7 @@
 
         return (jnp.where((odd == 1) & (k >= 2), k + 2, k), pos0[0, k], pos0[1, k], True)
 
-    def spilled_of(k, parts=both):
+    def spilled_of(k, parts=range(4)):
         for c in parts:
             spill_copy(k, c).wait_recv()
         return (k + 10, pos1[0, k], pos1[1, k], False)
@@ -484,14 +486,15 @@
 
     @pl.when(odd == 0)
     def _():
-        for c in both:
+        for c in parts:
             send_back(first, c)
             send_back(second, c)
         send_back(across, 0)
-
-    @pl.when(odd == 1)
-    def _():
-        for c in both:
+        send_back(across, 1)
+
+    @pl.when(odd == 1)
+    def _():
+        for c in parts:
             send_back(first, c)
             send_back(second, c)
 
@@ -499,10 +502,10 @@
 
     @pl.when(odd == 1)
     def _():
-        for c in both:
+        for c in parts:
             g_copy(first, c).wait_send()
             g_copy(second, c).wait_send()
-        for c in both:
+        for c in parts:
             send_back(across, c)
 
     pass_on(first)
@@ -513,7 +516,8 @@
         add_pieces(canvas, pool, [mine_of(d)])
         add_pieces(canvas, pool, [mine_of(first), mine_of(second)])
         pl.semaphore_wait(turn_sem.at[1], 1)
-        send_back(across, 1)
+        send_back(across, 2)
+        send_back(across, 3)
         add_pieces(canvas, pool, [spilled_of(d), spilled_of(first), spilled_of(second)])
         pass_on(across)
 
@@ -521,13 +525,14 @@
     def _():
         add_pieces(canvas, pool, [mine_of(d)])
         g_copy(across, 0).wait_send()
+        g_copy(across, 1).wait_send()
         pl.semaphore_signal(turn_sem.at[1], inc=1, device_id=(d, t - 1), device_id_type=MESH)
         add_pieces(canvas, pool, [spilled_of(d), spilled_of(first), spilled_of(second)])
         pass_on(across)
         add_pieces(canvas, pool, [mine_of(first), mine_of(second)])
 
-    for c in both:
-        add_pieces(canvas, pool, [mine_of(across, (c,)), spilled_of(across, (c,))], (c,))
+    for part in parts:
+        add_pieces(canvas, pool, [mine_of(across, (part,)), spilled_of(across, (part,))], (part,))
 
     info1.wait_send()
 
@@ -541,23 +546,27 @@
         for c in both:
             for k in (2, 3):
                 far_copy(k, c).wait_send()
-                back_copy(k, c).wait_send()
             y_copy(first, c).wait_send()
             y_copy(second, c).wait_send()
         y_copy(across, 0).wait_send()
-        g_copy(across, 1).wait_send()
+        for part in parts:
+            back_copy(2, part).wait_send()
+            back_copy(3, part).wait_send()
+        g_copy(across, 2).wait_send()
+        g_copy(across, 3).wait_send()
 
     @pl.when(odd == 0)
     def _():
-        for c in both:
+        for part in parts:
             for k in (first, second, across):
-                g_copy(k, c).wait_send()
+                g_copy(k, part).wait_send()
 
     y_copy(across, 1).wait_send()
     for k in range(4):
         for c in both:
             halo_copy(k, c).wait_send()
-            spill_copy(k, c).wait_send()
+        for part in parts:
+            spill_copy(k, part).wait_send()
 
 
 def solution(mesh):
@@ -583,7 +592,7 @@
                 pltpu.VMEM(PIECE, F32),
                 pltpu.VMEM((2, 2, N, N), BF),
                 pltpu.VMEM((2, 2, N, N), BF),
-                pieces(14),
+                pltpu.VMEM((14, 4, H, N), F32),
                 pltpu.VMEM(tables.shape, BF),
                 pltpu.VMEM(order.shape, BF),
                 pltpu.VMEM((N, N), F32),
@@ -593,7 +602,7 @@
                 pltpu.SMEM((2, 4), jnp.int32),
                 pltpu.SMEM((2, 4), jnp.int32),
                 dma((4,)), dma((columns // H,)), dma((2,)), dma((2,)), dma((4, 2)), dma((4, 2)), dma((2, 2)), dma((2, 2)),
-                dma((4, 2)), dma((4, 2)), dma((4, 2)), dma((4, 2)), dma((4, 2)), dma((4, 2)), dma((2, 2)), dma((2, 2)),
+                dma((4, 2)), dma((4, 2)), dma((4, 4)), dma((4, 4)), dma((4, 4)), dma((4, 4)), dma((2, 4)), dma((2, 4)),
                 dma(()), dma(()), pltpu.SemaphoreType.REGULAR((2,)),
             ],
             compiler_params=pltpu.CompilerParams(

time: 72.2 us -> 71.7 us (level)
  no operation moved by 1% of the time
where the time goes in v4:
time: 71.7 us; the launch traced here: 71.6 us
  Pallas kernels  68.2 us (95%)
  local copies, waits for them, and re-layouts  3.4 us (5%)
    pallas_call x1, Pallas kernels, local(): pl.pallas_call(functools.partial(gradient_kernel, depth, tiles), out_shap...  68.2 us
    unnamed x1, local copies, waits for them, and re-layouts  3.4 us

profile of v4, /device:TPU:1, one launch (start us, length us, event | category | flops | bytes accessed | tf_op | source)
XLA Modules:
  0.0 71.6 jit_solution(16606059301171910822)
XLA Ops:
  0.0 68.2 %shard_map.73 = f32[2,256,4096]{2,1,0:T(8,128)S(1)} custom-call(f32[2,1,256,4096]{3,2,1,0:T(8,128)} %specimen.1, s32[2,4]{1,0:T(2,128)} %positions.1, s32[4]{0:T(128)} %occupied.1, f32[4,256,256]{2,1,0:T(8,128)} %measured.1, f32[2,256,256]{2,1,0:T(8,128)} %probe.1, bf16[2,3,2,2,256,256]{5,4,3,2,1,0:T(8,128)(2,1)} %constant.4.clone.tables, ...), custom_call_target="tpu_custom_call" | custom-call | tf_op jit(solution)/shard_map/pallas_call | solution.py:584
  68.2 3.4 %copy.10 = f32[2,1,256,4096]{3,2,1,0:T(8,128)} copy(f32[2,1,256,4096]{3,2,1,0:T(8,128)S(1)} %bitcast.3) | data formatting | bytes 16777216
